TPU v7x, 32 devices: a whole 2x2x4 slice. The times are simulated.
32 devices in a mesh: grp: 2 (over y), fac: 16 (over z, x, core).
Axes of the slice: x: 2, y: 2, z: 4, core: 2. Of those that a mesh axis runs over, the one named last changes fastest.
Arguments:
- lattice_gen: int32 [2, 4096], P(None, 'fac'), may hold values from 1 to 65535
- lattice_shift: int32 [2, 32, 4096], P(None, 'grp', 'fac'), parts along dimension 1, may hold values from 0 to 65535
- loading: bfloat16 [4096, 4096], P('fac'), as said below
- basis_proj: bfloat16 [4096, 256], P('fac'), may hold values from -0.09375 to 0.09375
- basis_bias: float32 [256], replicated, may hold values from -3 to 3
- trade_block: int32 [10240], P(('grp', 'fac')), parts along dimension 0, may hold values from 0 to 31
- trade_weights: float32 [10240, 8], P(('grp', 'fac')), parts along dimension 0, may hold values from -2 to 2
- trade_notional: float32 [10240], P(('grp', 'fac')), parts along dimension 0, may hold values from -2.4 to 2.4
- trade_strike: float32 [10240], P(('grp', 'fac')), parts along dimension 0, may hold values from 0.6 to 1.6
- trade_owner: int32 [10240, 1], P(('grp', 'fac')), parts along dimension 0, may hold values from 0 to 15; in each aligned block of 320 rows (0 to 319, 320 to 639, ...) at most 40 rows name the same one
- trade_slot: int32 [10240], P(('grp', 'fac')), parts along dimension 0, may hold values from 0 to 23
Outputs:
- fitted: float32 [2, 384, 2048], P(None, 'fac', 'grp'), parts along dimension 2
- exposure: float32 [384, 4], P('fac', 'grp'), parts along dimension 1
There are 2 independent parts, one for each index of `grp`. A program takes and returns all parts, laid end to end along the dimension named above; an argument that names none is the same for every part. Nothing has to cross between parts.
Inputs may be any that keep to these rules, and one draw needn't show every extreme that they name: `trade_owner`: among the trades of one index of fac no owner is named by more than 40 trades, a bound that some block reaches. `loading`: zero above the diagonal, 0.5 on it.
All inputs are finite; a program needn't handle non-finite values.
Results may differ from a plain program's by a relative error of at most 0.003.
Values may be sent and summed in bfloat16 or wider, within the bound.
A program may use at most 64 MiB of HBM per device.

v0:
```python
import jax
import jax.numpy as jnp
from jax import lax
from jax.sharding import PartitionSpec as P

BLOCK = 8
LATTICE = 65536
REPLICAS = 16
POINTS = 64
NSET_DEV = 24


drift_rate = 0.25
ridge_term = 0.01
keep_share = 0.8
new_share = 0.6
root_two = 1.4142135623730951


def lattice_normals(lattice_gen, lattice_shift):
    points = jnp.arange(POINTS, dtype=jnp.int32)
    offsets = jnp.transpose(lattice_shift, (0, 2, 1))
    index = (
        points[None, None, None, :] * lattice_gen[:, :, None, None] + offsets[:, :, :, None]
    ) % LATTICE
    unit = (index.astype(jnp.float32) + 0.5) / LATTICE
    normal = root_two * lax.erf_inv(2.0 * unit - 1.0)
    return normal.reshape(lattice_gen.shape[0], lattice_gen.shape[1], REPLICAS * POINTS).astype(
        jnp.bfloat16
    )


def local(
    lattice_gen,
    lattice_shift,
    loading,
    basis_proj,
    basis_bias,
    trade_block,
    trade_weights,
    trade_notional,
    trade_strike,
    trade_owner,
    trade_slot,
):
    high = lax.Precision.HIGHEST
    own_rows = loading.shape[0]
    scenarios = REPLICAS * POINTS
    own_normals = lattice_normals(lattice_gen, lattice_shift)
    mixed = jnp.einsum(
        "gf,tfs->tgs",
        loading,
        lax.all_gather(own_normals, "fac", axis=1, tiled=True),
        preferred_element_type=jnp.float32,
    )
    state = jnp.stack([mixed[0], keep_share * mixed[0] + new_share * mixed[1]]).astype(jnp.bfloat16)
    partial_args = jnp.einsum("tgs,gk->tsk", state, basis_proj, preferred_element_type=jnp.float32)
    identity = ridge_term * jnp.eye(basis_proj.shape[1], dtype=jnp.float32)[None]
    arguments = lax.psum(partial_args, "fac")
    phi = jnp.tanh(arguments + basis_bias[None, None, :])
    gram = jnp.einsum("tsk,tsl->tkl", phi, phi, precision=high) / scenarios + identity
    block_count = own_rows // BLOCK
    blocks = state[1].astype(jnp.float32).reshape(block_count, BLOCK, scenarios)
    picker = (trade_block[:, None] == jnp.arange(block_count, dtype=jnp.int32)[None, :]).astype(
        jnp.float32
    )
    driver = jnp.zeros((trade_block.shape[0], scenarios), jnp.float32)
    for column in range(BLOCK):
        driver = driver + trade_weights[:, column : column + 1] * jnp.dot(
            picker, blocks[:, column, :], precision=high
        )
    value = (
        trade_notional[:, None] * (jnp.exp(drift_rate * driver) - trade_strike[:, None])
    ).astype(jnp.bfloat16)
    owner = trade_owner[:, 0]
    sets = owner * NSET_DEV + trade_slot
    member = (
        sets[None, :] == jnp.arange(NSET_DEV * lax.axis_size("fac"), dtype=jnp.int32)[:, None]
    ).astype(jnp.bfloat16)
    netting = lax.psum_scatter(
        jnp.dot(member, value, preferred_element_type=jnp.float32),
        "fac",
        scatter_dimension=0,
        tiled=True,
    )
    rhs = jnp.einsum("tsk,ns->tkn", phi, netting, precision=high) / scenarios
    factor = jnp.linalg.cholesky(gram)
    middle = lax.linalg.triangular_solve(factor, rhs, left_side=True, lower=True)
    coeffs = lax.linalg.triangular_solve(
        factor, middle, left_side=True, lower=True, transpose_a=True
    )
    fitted = jnp.einsum("tkn,tsk->tns", coeffs, phi, precision=high)
    exposure = jnp.mean(jnp.maximum(fitted, 0.0), axis=2).T
    return (fitted, exposure)


def solution(mesh):
    return jax.shard_map(
        local,
        mesh=mesh,
        in_specs=(
            P(None, "fac"),
            P(None, "grp", "fac"),
            P("fac", None),
            P("fac", None),
            P(),
            P(("grp", "fac")),
            P(("grp", "fac"), None),
            P(("grp", "fac")),
            P(("grp", "fac")),
            P(("grp", "fac"), None),
            P(("grp", "fac")),
        ),
        out_specs=(P(None, "fac", "grp"), P("fac", "grp")),
        check_vma=False,
    )
```

profile of v0, /device:TPU:27, one launch (start us, length us, event | category | flops | bytes accessed | tf_op | source)
XLA Modules:
  0.0 392.1 jit_solution(15190659263221404019)
XLA Ops:
  7.2 0.8 iota_multiply_fusion
  8.1 2.3 broadcast_add_fusion
  10.4 2.9 copy.45
  13.3 6.8 %multiply_convert_fusion = bf16[2,256,1024]{2,1,0:T(8,128)(2,1)} fusion(s32[2,256,1024]{2,1,0:T(8,128)} %copy.45), kind=kLoop, calls=%fused_computation.16 | loop fusion | flops 28311552 | bytes 3145728 | tf_op jit(solution)/shard_map/convert_element_type | solution.py:28
  23.5 122.2 %all-gather.2.cloned.1.call-done = bf16[2,4096,1024]{2,1,0:T(8,128)(2,1)} async-done(((bf16[2,256,1024]{2,1,0:T(8,128)(2,1)}), bf16[2,4096,1024]{2,1,0:T(8,128)(2,1)}) %all-gather.2.cloned.1.call-update) | async-done | bytes 16777232 | tf_op jit(solution)/shard_map/all_gather | solution.py:53
  145.7 8.1 %fusion.10 = f32[2,256,1024]{2,1,0:T(8,128)S(1)} fusion(bf16[2,4096,1024]{2,1,0:T(8,128)(2,1)} %all-gather.2.cloned.1.call-done, bf16[256,4096]{1,0:T(8,128)(2,1)S(1)} %copy-done), kind=kOutput, calls=%fused_computation.19 | convolution fusion | flops 4294967296 | bytes 20971520 | tf_op jit(solution)/shard_map/gf,tfs->tgs/dot_general | solution.py:50
  154.3 1.6 fusion.71
  155.9 1.8 fusion.32
  158.4 1.0 fusion.26
  162.2 1.8 fusion.39
  163.9 89.6 %all-reduce.3.cloned.1.call-done = f32[2,1024,256]{2,1,0:T(8,128)} async-done(((f32[2,1024,256]{2,1,0:T(8,128)}), f32[2,1024,256]{2,1,0:T(8,128)}) %all-reduce.3.cloned.1.call-update) | async-done | bytes 2097168 | tf_op jit(solution)/shard_map/psum | solution.py:59
  253.6 6.7 %broadcast_add_fusion.1 = (f32[2,256,256]{1,2,0:T(8,128)}, f32[2,256,256]{1,2,0:T(8,128)S(1)}) fusion(f32[256,256]{0,1:T(8,128)S(1)} %copy.51, f32[2,1024,256]{2,1,0:T(8,128)} %all-reduce.3.cloned.1.call-done, f32[256]{0:T(256)S(1)} %copy-done.10), kind=kOutput, calls=%fused_computation.68 | convolution fusion | flops 1611399168 | bytes 3408896 | tf_op jit(solution)/shard_map/tsk,tsl->tkl/dot_general | solution.py:61
  260.3 1.2 copy.52
  262.5 23.7 %custom-call.18 = f32[2,128,128]{2,1,0:T(8,128)S(1)} custom-call(f32[2,128,128]{2,1,0:T(8,128)S(1)} %cholesky.122), custom_call_target="Cholesky" | custom-call | tf_op jit(solution)/shard_map/jit(cholesky)/cholesky | solution.py:87
  286.2 19.7 %custom-call.19 = f32[2,1,128,128]{2,3,1,0:T(8,128)S(1)} custom-call(f32[2,1,128,128]{3,2,1,0:T(8,128)S(1)} %select_bitcast_fusion), custom_call_target="InvertDiagBlocksLowerTriangular" | custom-call | tf_op jit(solution)/shard_map/jit(cholesky)/cholesky | solution.py:87
  305.9 1.2 constant_dynamic-update-slice_fusion.1
  307.1 1.3 convolution_subtract_fusion
  308.4 23.5 %custom-call.20 = f32[2,128,128]{2,1,0:T(8,128)S(1)} custom-call(f32[2,128,128]{2,1,0:T(8,128)S(1)} %convolution_subtract_fusion), custom_call_target="Cholesky" | custom-call | tf_op jit(solution)/shard_map/jit(cholesky)/cholesky | solution.py:87
  332.3 5.2 %while.1 = (s32[]{:T(128)}, f32[2,256,256]{2,1,0:T(8,128)S(1)}, s32[2,2]{1,0:T(2,128)S(1)}, f32[2,2,128,128]{3,2,0,1:T(8,128)}, s32[]{:T(128)}) while((s32[]{:T(128)}, f32[2,256,256]{2,1,0:T(8,128)S(1)}, s32[2,2]{1,0:T(2,128)S(1)}, f32[2,2,128,128]{3,2,0,1:T(8,128)}, s32[]{:T(128)}) %tuple.43), condition=%wide.while_cond, body=%wide.while_body.sunk | while | flops 2 | bytes 263777 | solution.py:89
  332.9 2.0 bitcast_dynamic-update-slice_fusion.2
  335.5 2.0 bitcast_dynamic-update-slice_fusion.2
  337.6 40.1 %custom-call.21 = f32[2,2,128,128]{2,3,1,0:T(8,128)S(1)} custom-call(f32[2,2,128,128]{3,2,1,0:T(8,128)} %bitcast.90), custom_call_target="InvertDiagBlocksLowerTriangular" | custom-call | tf_op jit(solution)/shard_map/triangular_solve | solution.py:89
  377.7 3.1 fusion.29
  382.5 2.5 maximum_reduce_fusion
  (90 shorter events, 11.9 us)
Async XLA Ops:
  7.2 138.5 %copy-start = (bf16[256,4096]{1,0:T(8,128)(2,1)S(1)}, bf16[256,4096]{1,0:T(8,128)(2,1)}, u32[]{:S(2)}) copy-start(bf16[256,4096]{1,0:T(8,128)(2,1)} %param.13) | copy-start | bytes 6291460
  7.2 138.5 %all-gather.2.cloned.1.call-start = ((), (), s32[]{:S(2)}) async-start(), calls=%async_computation.1 | async-start | bytes 17825792 | tf_op jit(solution)/shard_map/all_gather | solution.py:53
  13.3 7.1 %copy-start.17 = (s32[320,1]{0,1:T(1,128)S(1)}, s32[320,1]{0,1:T(1,128)}, u32[]{:S(2)}) copy-start(s32[320,1]{0,1:T(1,128)} %param.20) | copy-start | bytes 3844
  13.3 7.1 %copy-start.16 = (s32[320]{0:T(512)S(1)}, s32[320]{0:T(512)}, u32[]{:S(2)}) copy-start(s32[320]{0:T(512)} %param.21) | copy-start | bytes 3844
  13.3 9.5 %copy-start.9 = (f32[320,8]{0,1:T(8,128)S(1)}, f32[320,8]{0,1:T(8,128)}, u32[]{:S(2)}) copy-start(f32[320,8]{0,1:T(8,128)} %param.17) | copy-start | bytes 30724
  20.1 233.4 %all-reduce.3.cloned.1.call-start = ((), (), s32[]{:S(2)}) async-start(), calls=%async_computation.2 | async-start | bytes 4194304 | tf_op jit(solution)/shard_map/psum | solution.py:59
  154.2 1.7 copy-start.4
  155.9 2.1 copy-start.6
  157.7 220.0 %reduce-scatter.2.cloned.1.call-start = ((), (), s32[]{:S(2)}) async-start(), calls=%async_computation.3 | async-start | bytes 1671168 | tf_op jit(solution)/shard_map/reduce_scatter | solution.py:80
  158.0 1.5 copy-start.14
  158.4 1.5 copy-start.13
  159.5 0.8 copy-start.12
  159.9 0.8 copy-start.11
  160.7 0.9 copy-start.5
  160.7 0.9 copy-start.15
  160.7 0.9 copy-start.18
  160.7 0.9 copy-start.19
  162.1 91.4 %copy-start.10 = (f32[256]{0:T(256)S(1)}, f32[256]{0:T(256)}, u32[]{:S(2)}) copy-start(f32[256]{0:T(256)} %param.15) | copy-start | bytes 3076
  260.3 25.9 %copy-start.8 = (pred[128,128]{1,0:T(8,128)(4,1)S(1)}, pred[128,128]{1,0:T(8,128)(4,1)}, u32[]{:S(2)}) copy-start(pred[128,128]{1,0:T(8,128)(4,1)} %iota_compare_fusion.14) | copy-start | bytes 49156
  261.5 70.3 %copy-start.7 = (pred[128,128]{1,0:T(8,128)(4,1)S(1)}, pred[128,128]{1,0:T(8,128)(4,1)}, u32[]{:S(2)}) copy-start(pred[128,128]{1,0:T(8,128)(4,1)} %iota_compare_fusion.15) | copy-start | bytes 49156
  261.6 70.5 %copy-start.3 = (pred[256,256]{1,0:T(8,128)(4,1)S(1)}, pred[256,256]{1,0:T(8,128)(4,1)}, u32[]{:S(2)}) copy-start(pred[256,256]{1,0:T(8,128)(4,1)} %iota_compare_fusion.4) | copy-start | bytes 196612
  261.7 0.8 copy-start.2
  262.5 69.8 %copy-start.20 = (s32[2]{0:T(128)S(1)}, s32[2]{0:T(128)}, u32[]{:S(2)}) copy-start(s32[2]{0:T(128)} %iota_multiply_fusion.1) | copy-start | bytes 28
  377.7 4.8 %copy-start.1 = (f32[2,1024,256]{2,1,0:T(8,128)S(1)}, f32[2,1024,256]{2,1,0:T(8,128)}, u32[]{:S(2)}) copy-start(f32[2,1024,256]{2,1,0:T(8,128)} %all-reduce.3.cloned.1.call-done) | copy-start | bytes 6291460
Sparse Core Ops, SparseCore 0:
  20.3 125.3 all-gather.1
  157.9 95.6 all-reduce.2
  257.7 58.2 reduce-scatter.1
where the time goes:
time: 397 us; the launch traced here: 392 us
  waiting for transfers between devices  212 us (53%)
  other arithmetic  121 us (30%)
  matrix products  32 us (8%)
  between operations  14.2 us (4%)
  local copies, waits for them, and re-layouts  12.9 us (3%)
    all_gather x1, waiting for transfers between devices, local(): lax.all_gather(own_normals, 'fac', axis=1, tiled=True)  122 us
    psum x1, waiting for transfers between devices, local(): arguments = lax.psum(partial_args, 'fac')  89.6 us
    another operation x9, other arithmetic, local(): factor = jnp.linalg.cholesky(gram)  68.2 us
    another operation x4, other arithmetic, local(): lax.linalg.triangular_solve(factor, middle, left_side=True, lower=True, t...  41.4 us
    dot_general x1, matrix products, local(): jnp.einsum('gf,tfs->tgs', loading, lax.all_gather(own_normals, 'fac', axi...  8.11 us
  transfers between devices with their start and end apart: 3, of which 2 were waited for; matrix products, arithmetic and copies ran while one was open for 34% of the time, Pallas kernels for 0%

commit v1 on v0

v1 whole, which is shorter than its diff:
```python
import functools
import math

import jax
import jax.numpy as jnp
from jax import lax
from jax.experimental import pallas as pl
from jax.experimental.pallas import tpu as pltpu
from jax.sharding import PartitionSpec as P

BLOCK = 8
LATTICE = 65536
REPLICAS = 16
POINTS = 64
NSET_DEV = 24
SET_ROWS = 32
SHARE = 2
SCENARIOS = REPLICAS * POINTS
LOCAL = SCENARIOS // SHARE
LOCAL_REPLICAS = REPLICAS // SHARE
LINES = 1 + LOCAL_REPLICAS

drift_rate = 0.25
ridge_term = 0.01
keep_share = 0.8
new_share = 0.6

VMEM_LIMIT = 56 * 1024 * 1024
HIGH = lax.Precision.HIGHEST
MESH = pl.DeviceIdType.MESH

LOG_SCALE = -2.0 / (15.001 * math.log(2.0))
NORMAL_TERMS = (
    3.00101966e00,
    1.55010142e00,
    -2.74155082e-01,
    3.36067480e-02,
    4.31695681e-02,
    -5.08279578e-02,
    3.10899462e-02,
    -1.21453725e-03,
    -1.43043690e-02,
    4.24694167e-03,
    2.40633730e-03,
)

INVERSE_STEPS = 11


def greet(me, n):
    barrier = pltpu.get_barrier_semaphore()
    for step in range(1, n):
        pl.semaphore_signal(
            barrier, inc=1, device_id={"fac": lax.rem(me + step, n)}, device_id_type=MESH
        )
    pl.semaphore_wait(barrier, n - 1)


def remote(src, dst, send, recv, peer):
    return pltpu.make_async_remote_copy(
        src_ref=src,
        dst_ref=dst,
        send_sem=send,
        recv_sem=recv,
        device_id={"fac": peer},
        device_id_type=MESH,
    )


def share_kernel(n, lines, load, proj, trade, lines_out, load_out, proj_out, trade_out, sends, recvs, mate_sends, mate_recvs, own):
    me = lax.axis_index("fac")
    core = lax.rem(me, SHARE)
    mate = me + 1 - 2 * core
    greet(me, n)
    copies = []
    for step in range(1, n):
        peer = lax.rem(me + step, n)
        copies.append(
            remote(lines.at[lax.rem(peer, SHARE)], lines_out.at[me], sends.at[step], recvs.at[step], peer)
        )
    for index, (src, dst) in enumerate(((trade, trade_out), (proj, proj_out), (load, load_out))):
        copies.append(remote(src, dst, mate_sends.at[index], mate_recvs.at[index], mate))
    for copy in copies:
        copy.start()
    keep = pltpu.make_async_copy(lines.at[core], lines_out.at[me], own)
    keep.start()
    keep.wait()
    for copy in copies:
        copy.wait()


def share(lines, load, proj, trade, n):
    hbm = pl.BlockSpec(memory_space=pl.ANY)
    return pl.pallas_call(
        functools.partial(share_kernel, n),
        out_shape=(
            jax.ShapeDtypeStruct((n,) + lines.shape[1:], lines.dtype),
            jax.ShapeDtypeStruct(load.shape, load.dtype),
            jax.ShapeDtypeStruct(proj.shape, proj.dtype),
            jax.ShapeDtypeStruct(trade.shape, trade.dtype),
        ),
        in_specs=[hbm] * 4,
        out_specs=[hbm] * 4,
        scratch_shapes=[
            pltpu.SemaphoreType.DMA((n,)),
            pltpu.SemaphoreType.DMA((n,)),
            pltpu.SemaphoreType.DMA((3,)),
            pltpu.SemaphoreType.DMA((3,)),
            pltpu.SemaphoreType.DMA,
        ],
        compiler_params=pltpu.CompilerParams(collective_id=0, has_side_effects=True),
    )(lines, load, proj, trade)


def mix_kernel(lines, load_own, load_mate, proj_own, proj_mate, trade_own, trade_mate, args, net, normal, base, mixed):
    step = pl.program_id(0)
    width = lines.shape[1]
    rows = load_own.shape[0]
    tile = 16

    @pl.when(step == 0)
    def _():
        mixed[...] = jnp.zeros_like(mixed)

    for t in range(2):
        base[...] = lax.broadcasted_iota(jnp.int32, (POINTS, width), 0) * lines[t * LINES : t * LINES + 1, :]

        def replica(r, carry):
            shift = lines[pl.ds(t * LINES + 1 + r, 1), :]
            for part in range(POINTS // tile):
                index = (base[part * tile : (part + 1) * tile, :] + shift) & (LATTICE - 1)
                x = index.astype(jnp.float32) * (2.0 / LATTICE) + (1.0 / LATTICE - 1.0)
                power = jnp.log((1.0 - x) * (1.0 + x)) * LOG_SCALE - 1.0
                ratio = power * NORMAL_TERMS[-1] + NORMAL_TERMS[-2]
                for term in NORMAL_TERMS[-3::-1]:
                    ratio = ratio * power + term
                start = pl.multiple_of(t * LOCAL + r * POINTS + part * tile, tile)
                normal[pl.ds(start, tile), :] = (ratio * x).astype(jnp.bfloat16)
            return carry

        lax.fori_loop(0, LOCAL_REPLICAS, replica, 0)

    def multiply(m, carry):
        span = pl.ds(pl.multiple_of(m * 256, 256), 256)
        left = normal[span, :]
        for half, load in enumerate((load_own, load_mate)):
            mixed[half, span, :] += lax.dot_general(
                left, load[...], (((1,), (1,)), ((), ())), preferred_element_type=jnp.float32
            )
        return carry

    lax.fori_loop(0, 2 * LOCAL // 256, multiply, 0)

    @pl.when(step == pl.num_programs(0) - 1)
    def _():
        picks = []
        members = []
        n_rows = net.shape[0] * SET_ROWS
        for trade in (trade_own, trade_mate):
            weights = jnp.concatenate([trade[0:8, :]] * (rows // BLOCK), axis=0)
            home = lax.shift_right_logical(lax.broadcasted_iota(jnp.int32, weights.shape, 0), 3)
            pick = jnp.where(home == trade[8:9, :].astype(jnp.int32), weights, 0.0)
            parts = []
            for _ in range(3):
                part = pick.astype(jnp.bfloat16)
                parts.append(part)
                pick = pick - part.astype(jnp.float32)
            picks.append(parts)
            sets = trade[11:12, :].astype(jnp.int32)
            members.append(
                jnp.where(lax.broadcasted_iota(jnp.int32, (n_rows, sets.shape[1]), 0) == sets, 1.0, 0.0).astype(jnp.bfloat16)
            )
        chunk = 128
        for m in range(LOCAL // chunk):
            low = slice(m * chunk, (m + 1) * chunk)
            high = slice(LOCAL + m * chunk, LOCAL + (m + 1) * chunk)
            totals = [0.0, 0.0]
            sums = 0.0
            for half, (proj, trade) in enumerate(((proj_own, trade_own), (proj_mate, trade_mate))):
                first = mixed[half, low, :]
                second = mixed[half, high, :]
                state = [
                    first.astype(jnp.bfloat16),
                    (keep_share * first + new_share * second).astype(jnp.bfloat16),
                ]
                for t in range(2):
                    totals[t] = totals[t] + jnp.dot(state[t], proj[...], preferred_element_type=jnp.float32)
                driver = 0.0
                for part in picks[half]:
                    driver = driver + jnp.dot(state[1], part, preferred_element_type=jnp.float32)
                value = (trade[9:10, :] * (jnp.exp(drift_rate * driver) - trade[10:11, :])).astype(jnp.bfloat16)
                sums = sums + lax.dot_general(
                    members[half], value, (((1,), (1,)), ((), ())), preferred_element_type=jnp.float32
                )
            for t in range(2):
                args[t, low, :] = totals[t]
            net[:, :, low] = sums.astype(jnp.bfloat16).reshape(net.shape[0], SET_ROWS, chunk)


def mix(lines, load_own, load_mate, proj_own, proj_mate, trade_own, trade_mate, n):
    rows, factors = load_own.shape
    width = 512
    basis = proj_own.shape[1]
    fixed = lambda j: (0, 0)
    return pl.pallas_call(
        mix_kernel,
        grid=(factors // width,),
        out_shape=(
            jax.ShapeDtypeStruct((2, LOCAL, basis), jnp.float32),
            jax.ShapeDtypeStruct((n, SET_ROWS, LOCAL), jnp.bfloat16),
        ),
        in_specs=[
            pl.BlockSpec((lines.shape[0], width), lambda j: (0, j)),
            pl.BlockSpec((rows, width), lambda j: (0, j)),
            pl.BlockSpec((rows, width), lambda j: (0, j)),
            pl.BlockSpec(proj_own.shape, fixed),
            pl.BlockSpec(proj_own.shape, fixed),
            pl.BlockSpec(trade_own.shape, fixed),
            pl.BlockSpec(trade_own.shape, fixed),
        ],
        out_specs=(
            pl.BlockSpec((2, LOCAL, basis), lambda j: (0, 0, 0)),
            pl.BlockSpec((n, SET_ROWS, LOCAL), lambda j: (0, 0, 0)),
        ),
        scratch_shapes=[
            pltpu.VMEM((2 * LOCAL, width), jnp.bfloat16),
            pltpu.VMEM((POINTS, width), jnp.int32),
            pltpu.VMEM((2, 2 * LOCAL, rows), jnp.float32),
        ],
        compiler_params=pltpu.CompilerParams(vmem_limit_bytes=VMEM_LIMIT),
    )(lines, load_own, load_mate, proj_own, proj_mate, trade_own, trade_mate)


def reduce_kernel(n, args, bias, net, phi, net_out, args_in, arg_sends, arg_recvs, net_sends, net_recvs, phi_sends, phi_recvs, mate_sends, mate_recvs, own):
    me = lax.axis_index("fac")
    core = lax.rem(me, SHARE)
    pair = lax.div(me, SHARE)
    mate = me + 1 - 2 * core
    pairs = n // SHARE
    block = LOCAL // pairs
    greet(me, n)

    def part(index):
        return pl.ds(pl.multiple_of(index * block, 8), block)

    def place(index, side):
        return pl.ds(pl.multiple_of(side * LOCAL + index * block, 8), block)

    arg_copies = []
    for step in range(1, pairs):
        other = lax.rem(pair + step, pairs)
        arg_copies.append(
            remote(args.at[:, part(other), :], args_in.at[pair], arg_sends.at[step], arg_recvs.at[step], SHARE * other + core)
        )
    net_copies = []
    for step in range(1, n):
        peer = lax.rem(me + step, n)
        net_copies.append(remote(net.at[peer], net_out.at[me], net_sends.at[step], net_recvs.at[step], peer))
    for copy in arg_copies + net_copies:
        copy.start()
    keep = pltpu.make_async_copy(net.at[me], net_out.at[me], own)
    keep.start()
    total = args[:, part(pair), :] + bias[...][None]
    for copy in arg_copies:
        copy.wait_recv()
    for step in range(1, pairs):
        total = total + args_in[lax.rem(pair + step, pairs)]
    mine = place(pair, core)
    phi[:, mine, :] = jnp.tanh(total)
    phi_copies = []
    for step in range(1, pairs):
        other = lax.rem(pair + step, pairs)
        phi_copies.append(
            remote(phi.at[:, mine, :], phi.at[:, mine, :], phi_sends.at[step], phi_recvs.at[step], SHARE * other + core)
        )
    mate_copies = [remote(phi.at[:, mine, :], phi.at[:, mine, :], mate_sends.at[0], mate_recvs.at[0], mate)]
    for copy in phi_copies + mate_copies:
        copy.start()
    for step in range(1, pairs):
        phi_copies[step - 1].wait_recv()
        there = place(lax.rem(pair - step + pairs, pairs), core)
        forward = remote(phi.at[:, there, :], phi.at[:, there, :], mate_sends.at[step], mate_recvs.at[step], mate)
        forward.start()
        mate_copies.append(forward)
    keep.wait()
    for copy in net_copies:
        copy.wait_recv()
    for copy in mate_copies:
        copy.wait_recv()
    for copy in arg_copies + net_copies + phi_copies + mate_copies:
        copy.wait_send()


def reduce(args, bias, net):
    n = net.shape[0]
    pairs = n // SHARE
    block = LOCAL // pairs
    basis = args.shape[2]
    vmem = pl.BlockSpec(memory_space=pltpu.VMEM)
    sems = [pltpu.SemaphoreType.DMA((k,)) for k in (pairs, pairs, n, n, pairs, pairs, pairs, pairs)]
    return pl.pallas_call(
        functools.partial(reduce_kernel, n),
        out_shape=(
            jax.ShapeDtypeStruct((2, SCENARIOS, basis), jnp.float32),
            jax.ShapeDtypeStruct(net.shape, net.dtype),
        ),
        in_specs=[vmem] * 3,
        out_specs=(vmem, vmem),
        scratch_shapes=[pltpu.VMEM((pairs, 2, block, basis), jnp.float32)] + sems + [pltpu.SemaphoreType.DMA],
        compiler_params=pltpu.CompilerParams(collective_id=1, has_side_effects=True, vmem_limit_bytes=VMEM_LIMIT),
    )(args, bias, net)


def regress_kernel(phi, net, fitted, exposure):
    n = net.shape[0]
    basis = phi.shape[2]
    sides = []
    for core in range(SHARE):
        side = net[core].astype(jnp.float32)
        for pair in range(1, n // SHARE):
            side = side + net[SHARE * pair + core].astype(jnp.float32)
        sides.append(side)
    netting = jnp.concatenate(sides, axis=1)
    eye = jnp.where(
        lax.broadcasted_iota(jnp.int32, (basis, basis), 0) == lax.broadcasted_iota(jnp.int32, (basis, basis), 1),
        1.0,
        0.0,
    )
    dot = functools.partial(jnp.dot, precision=HIGH, preferred_element_type=jnp.float32)
    grams = []
    rhs = []
    for t in range(2):
        basis_values = phi[t]
        grams.append(
            lax.dot_general(
                basis_values, basis_values, (((0,), (0,)), ((), ())), precision=HIGH, preferred_element_type=jnp.float32
            )
            * (1.0 / SCENARIOS)
            + ridge_term * eye
        )
        rhs.append(dot(netting, basis_values) * (1.0 / SCENARIOS))
    least, most = ridge_term, basis + ridge_term
    spread = (most - least) / (most + least)
    inverses = [eye * (2.0 / (most + least))] * 2
    for _ in range(INVERSE_STEPS):
        scale = 2.0 / (2.0 - spread * spread)
        spread = spread * spread / (2.0 - spread * spread)
        products = [dot(grams[t], inverses[t]) for t in range(2)]
        inverses = [scale * (2.0 * inverses[t] - dot(inverses[t], products[t])) for t in range(2)]
    for t in range(2):
        coeffs = dot(rhs[t], inverses[t])
        coeffs = coeffs + dot(rhs[t] - dot(coeffs, grams[t]), inverses[t])
        values = lax.dot_general(
            coeffs, phi[t], (((1,), (1,)), ((), ())), precision=HIGH, preferred_element_type=jnp.float32
        )[:NSET_DEV]
        fitted[t] = values
        exposure[:, t : t + 1] = jnp.sum(jnp.maximum(values, 0.0), axis=1, keepdims=True) * (1.0 / SCENARIOS)


def regress(phi, net):
    vmem = pl.BlockSpec(memory_space=pltpu.VMEM)
    return pl.pallas_call(
        regress_kernel,
        out_shape=(
            jax.ShapeDtypeStruct((2, NSET_DEV, SCENARIOS), jnp.float32),
            jax.ShapeDtypeStruct((NSET_DEV, 2), jnp.float32),
        ),
        in_specs=[vmem] * 2,
        out_specs=(vmem, vmem),
        compiler_params=pltpu.CompilerParams(vmem_limit_bytes=VMEM_LIMIT),
    )(phi, net)


def local(
    lattice_gen,
    lattice_shift,
    loading,
    basis_proj,
    basis_bias,
    trade_block,
    trade_weights,
    trade_notional,
    trade_strike,
    trade_owner,
    trade_slot,
):
    n = lax.axis_size("fac")
    factors = loading.shape[1]
    lines = jnp.concatenate(
        [
            jnp.concatenate(
                [lattice_gen[:, None, :], lattice_shift[:, side * LOCAL_REPLICAS : (side + 1) * LOCAL_REPLICAS, :]], axis=1
            ).reshape(1, 2 * LINES, -1)
            for side in range(SHARE)
        ],
        axis=0,
    )
    sets = trade_owner[:, 0] * SET_ROWS + trade_slot
    extra = jnp.stack([trade_block.astype(jnp.float32), trade_notional, trade_strike, sets.astype(jnp.float32)])
    trade = jnp.concatenate([trade_weights.T, extra, jnp.zeros_like(extra)], axis=0)
    all_lines, load_mate, proj_mate, trade_mate = share(lines, loading, basis_proj, trade, n)
    all_lines = jnp.transpose(all_lines, (1, 0, 2)).reshape(2 * LINES, factors)
    args, net = mix(all_lines, loading, load_mate, basis_proj, proj_mate, trade, trade_mate, n)
    phi, net = reduce(args, basis_bias[None, :], net)
    return regress(phi, net)


def solution(mesh):
    return jax.shard_map(
        local,
        mesh=mesh,
        in_specs=(
            P(None, "fac"),
            P(None, "grp", "fac"),
            P("fac", None),
            P("fac", None),
            P(),
            P(("grp", "fac")),
            P(("grp", "fac"), None),
            P(("grp", "fac")),
            P(("grp", "fac")),
            P(("grp", "fac"), None),
            P(("grp", "fac")),
        ),
        out_specs=(P(None, "fac", "grp"), P("fac", "grp")),
        check_vma=False,
    )
```

time: 397 us -> 153 us (0.39); the launches traced: 392 us -> 153 us
  waiting for transfers between devices: 212 us -> 0 us
  Pallas kernels: 0 us -> 141 us
  other arithmetic: 121 us -> 2.7 us
  matrix products: 32 us -> 0 us
  between operations: 14.2 us -> 0.68 us
  local copies, waits for them, and re-layouts: 12.9 us -> 8.18 us
    pallas_call x0 -> x4, Pallas kernels: none -> 141 us  [the longest x1 66.4 us: reduce(): pl.pallas_call(functools.partial(reduce_kernel, n), out_shape=(jax.ShapeD...]
    all_gather x1 -> x0, waiting for transfers between devices: 122 us -> none  [local(): lax.all_gather(own_normals, 'fac', axis=1, tiled=True)]
    another operation x13 -> x0, other arithmetic: 110 us -> none  [the longest x9 68.2 us: local(): factor = jnp.linalg.cholesky(gram)]
    psum x1 -> x0, waiting for transfers between devices: 89.6 us -> none  [local(): arguments = lax.psum(partial_args, 'fac')]
    dot_general x14 -> x0, matrix products: 27.8 us -> none  [the longest x1 8.11 us: local(): jnp.einsum('gf,tfs->tgs', loading, lax.all_gather(own_normals, 'fac', axi...]
    convert_element_type x1 -> x2, other arithmetic: 6.8 us -> 1.37 us  [the longest x1 0.69 us: local(): sets.astype(jnp.float32)]
    add x2 -> x0, local copies, waits for them, and re-layouts: 4.19 us -> none  [the longest x1 2.94 us: lattice_normals(): points[None, None, None, :] * lattice_gen[:, :, None, None]]
    another operation x8 -> x0, matrix products: 4.16 us -> none  [the longest x2 2.48 us: local(): factor = jnp.linalg.cholesky(gram)]
  transfers between devices with their start and end apart: 3 -> 0, of which waited for: 2 -> 0; matrix products, arithmetic and copies ran while one was open for 34% -> 0% of each run, Pallas kernels for 0% -> 0%
where the time goes in v1:
time: 153 us
  Pallas kernels  141 us (92%)
  local copies, waits for them, and re-layouts  8.18 us (5%)
  other arithmetic  2.7 us (2%)
    pallas_call x1, Pallas kernels, reduce(): pl.pallas_call(functools.partial(reduce_kernel, n), out_shape=(jax.ShapeD...  66.4 us
    pallas_call x1, Pallas kernels, mix(): pl.pallas_call(mix_kernel, grid=(factors // width,), out_shape=(jax.Shape...  39.7 us
    pallas_call x1, Pallas kernels, regress(): pl.pallas_call(regress_kernel, out_shape=(jax.ShapeDtypeStruct((2, NSET_D...  21.2 us
    pallas_call x1, Pallas kernels, share(): pl.pallas_call(functools.partial(share_kernel, n), out_shape=(jax.ShapeDt...  14 us

profile of v1, /device:TPU:27, one launch (start us, length us, event | category | flops | bytes accessed | tf_op | source)
XLA Modules:
  0.0 152.8 jit_solution(14217172906987626591)
XLA Ops:
  0.6 0.7 stack.13
  1.3 0.7 stack.14
  2.0 0.7 copy.15
  2.7 0.7 convert_element_type.6
  3.4 0.7 multiply_reduce_fusion
  4.1 0.7 add_convert_fusion
  4.8 1.9 %concatenate.15.trade.trade_own = f32[16,320]{1,0:T(8,128)} concatenate(f32[8,320]{1,0:T(8,128)} %bitcast.10, f32[1,320]{1,0:T(1,128)S(1)} %stack.12, f32[1,320]{1,0:T(1,128)S(1)} %stack.13, f32[1,320]{1,0:T(1,128)S(1)} %stack.14, f32[1,320]{1,0:T(1,128)S(1)} %stack.15, f32[4,320]{1,0:T(4,128)S(1)} %broadcast_in_dim.11), dimensions={0} | concatenate | bytes 40960 | tf_op jit(solution)/shard_map/concatenate | solution.py:400
  6.7 0.7 fusion
  7.5 0.6 pad_add_fusion.lines
  8.1 14.0 %shard_map.122 = (s32[16,18,256]{2,1,0:T(8,128)}, bf16[256,4096]{1,0:T(8,128)(2,1)}, bf16[256,256]{1,0:T(8,128)(2,1)}, f32[16,320]{1,0:T(8,128)}) custom-call(s32[2,18,256]{2,1,0:T(8,128)} %pad_add_fusion.lines, bf16[256,4096]{1,0:T(8,128)(2,1)} %load_own.1, bf16[256,256]{1,0:T(8,128)(2,1)} %proj_own.1, f32[16,320]{1,0:T(8,128)} %concatenate.15.trade.trade_own), custom_call_target="tpu_custom_call" | custom-call | tf_op jit(solution)/shard_map/pallas_call | solution.py:94
  22.1 1.1 copy.17
  23.2 1.0 copy.19
  24.2 39.7 %shard_map.123 = (f32[2,512,256]{2,1,0:T(8,128)}, bf16[16,32,512]{2,1,0:T(8,128)(2,1)}) custom-call(s32[18,4096]{1,0:T(8,128)} %bitcast.7, bf16[256,4096]{1,0:T(8,128)(2,1)} %load_own.1, bf16[256,4096]{1,0:T(8,128)(2,1)} %get-tuple-element.11.load_mate, bf16[256,256]{1,0:T(8,128)(2,1)} %proj_own.1, bf16[256,256]{1,0:T(8,128)(2,1)} %get-tuple-element.12.proj_mate, ...), custom_call_target="tpu_custom_call" | custom-call | tf_op jit(solution)/shard_map/pallas_call | solution.py:205
  63.9 66.4 %shard_map.124 = (f32[2,1024,256]{2,1,0:T(8,128)}, bf16[16,32,512]{2,1,0:T(8,128)(2,1)}) custom-call(f32[2,512,256]{2,1,0:T(8,128)} %get-tuple-element.14.args, f32[1,256]{1,0:T(1,128)} %bitcast.12, bf16[16,32,512]{2,1,0:T(8,128)(2,1)} %get-tuple-element.15.net), custom_call_target="tpu_custom_call" | custom-call | tf_op jit(solution)/shard_map/pallas_call | solution.py:301
  130.3 21.2 %shard_map.125 = (f32[2,24,1024]{2,1,0:T(8,128)}, f32[24,2]{1,0:T(8,128)}) custom-call(f32[2,1024,256]{2,1,0:T(8,128)} %get-tuple-element.16.phi, bf16[16,32,512]{2,1,0:T(8,128)(2,1)} %get-tuple-element.17.net), custom_call_target="tpu_custom_call" | custom-call | tf_op jit(solution)/shard_map/pallas_call | solution.py:362
  151.4 1.3 copy.18
  (7 shorter events, 0.1 us)

commit v2 on v1

--- a/solution.py
+++ b/solution.py
@@ -13,7 +13,6 @@
 REPLICAS = 16
 POINTS = 64
 NSET_DEV = 24
-SET_ROWS = 32
 SHARE = 2
 SCENARIOS = REPLICAS * POINTS
 LOCAL = SCENARIOS // SHARE
@@ -44,7 +43,18 @@
     2.40633730e-03,
 )
 
-INVERSE_STEPS = 11
+INVERSE_STEPS = 10
+
+CODES = 32767.0
+CHUNK = 128
+
+
+def encode(values):
+    return jnp.round(values).astype(jnp.int32).astype(jnp.int16)
+
+
+def decode(codes):
+    return codes.astype(jnp.int32).astype(jnp.float32)
 
 
 def greet(me, n):
@@ -67,7 +77,11 @@
     )
 
 
-def share_kernel(n, lines, load, proj, trade, lines_out, load_out, proj_out, trade_out, sends, recvs, mate_sends, mate_recvs, own):
+def share_kernel(n, *refs):
+    count = (len(refs) - 5) // 2
+    lines, *mine = refs[:count]
+    lines_out, *theirs = refs[count : 2 * count]
+    sends, recvs, mate_sends, mate_recvs, own = refs[2 * count :]
     me = lax.axis_index("fac")
     core = lax.rem(me, SHARE)
     mate = me + 1 - 2 * core
@@ -78,7 +92,7 @@
         copies.append(
             remote(lines.at[lax.rem(peer, SHARE)], lines_out.at[me], sends.at[step], recvs.at[step], peer)
         )
-    for index, (src, dst) in enumerate(((trade, trade_out), (proj, proj_out), (load, load_out))):
+    for index, (src, dst) in enumerate(zip(mine, theirs)):
         copies.append(remote(src, dst, mate_sends.at[index], mate_recvs.at[index], mate))
     for copy in copies:
         copy.start()
@@ -89,30 +103,30 @@
         copy.wait()
 
 
-def share(lines, load, proj, trade, n):
+def share(lines, arrays, n):
     hbm = pl.BlockSpec(memory_space=pl.ANY)
+    count = len(arrays)
     return pl.pallas_call(
         functools.partial(share_kernel, n),
-        out_shape=(
-            jax.ShapeDtypeStruct((n,) + lines.shape[1:], lines.dtype),
-            jax.ShapeDtypeStruct(load.shape, load.dtype),
-            jax.ShapeDtypeStruct(proj.shape, proj.dtype),
-            jax.ShapeDtypeStruct(trade.shape, trade.dtype),
-        ),
-        in_specs=[hbm] * 4,
-        out_specs=[hbm] * 4,
+        out_shape=[jax.ShapeDtypeStruct((n,) + lines.shape[1:], lines.dtype)]
+        + [jax.ShapeDtypeStruct(array.shape, array.dtype) for array in arrays],
+        in_specs=[hbm] * (count + 1),
+        out_specs=[hbm] * (count + 1),
         scratch_shapes=[
             pltpu.SemaphoreType.DMA((n,)),
             pltpu.SemaphoreType.DMA((n,)),
-            pltpu.SemaphoreType.DMA((3,)),
-            pltpu.SemaphoreType.DMA((3,)),
+            pltpu.SemaphoreType.DMA((count,)),
+            pltpu.SemaphoreType.DMA((count,)),
             pltpu.SemaphoreType.DMA,
         ],
         compiler_params=pltpu.CompilerParams(collective_id=0, has_side_effects=True),
-    )(lines, load, proj, trade)
-
-
-def mix_kernel(lines, load_own, load_mate, proj_own, proj_mate, trade_own, trade_mate, args, net, normal, base, mixed):
+    )(lines, *arrays)
+
+
+def mix_kernel(lines, *refs):
+    own, mate = refs[:8], refs[8:16]
+    codes, scale, net, normal, base, mixed, args = refs[16:]
+    load_own, load_mate = own[-1], mate[-1]
     step = pl.program_id(0)
     width = lines.shape[1]
     rows = load_own.shape[0]
@@ -155,28 +169,30 @@
     def _():
         picks = []
         members = []
-        n_rows = net.shape[0] * SET_ROWS
-        for trade in (trade_own, trade_mate):
-            weights = jnp.concatenate([trade[0:8, :]] * (rows // BLOCK), axis=0)
+        n_rows = net.shape[0] * NSET_DEV
+        for block, slot, owner, _, _, weight, _, _ in (own, mate):
+            weights = jnp.concatenate([weight[...]] * (rows // BLOCK), axis=0)
             home = lax.shift_right_logical(lax.broadcasted_iota(jnp.int32, weights.shape, 0), 3)
-            pick = jnp.where(home == trade[8:9, :].astype(jnp.int32), weights, 0.0)
+            pick = jnp.where(home == block[...], weights, 0.0)
             parts = []
             for _ in range(3):
                 part = pick.astype(jnp.bfloat16)
                 parts.append(part)
                 pick = pick - part.astype(jnp.float32)
             picks.append(parts)
-            sets = trade[11:12, :].astype(jnp.int32)
+            sets = owner[...] * NSET_DEV + slot[...]
             members.append(
                 jnp.where(lax.broadcasted_iota(jnp.int32, (n_rows, sets.shape[1]), 0) == sets, 1.0, 0.0).astype(jnp.bfloat16)
             )
-        chunk = 128
+        chunk = CHUNK
+        largest = 0.0
+        sums_of = []
         for m in range(LOCAL // chunk):
             low = slice(m * chunk, (m + 1) * chunk)
             high = slice(LOCAL + m * chunk, LOCAL + (m + 1) * chunk)
             totals = [0.0, 0.0]
             sums = 0.0
-            for half, (proj, trade) in enumerate(((proj_own, trade_own), (proj_mate, trade_mate))):
+            for half, (_, _, _, notional, strike, _, proj, _) in enumerate((own, mate)):
                 first = mixed[half, low, :]
                 second = mixed[half, high, :]
                 state = [
@@ -188,70 +204,71 @@
                 driver = 0.0
                 for part in picks[half]:
                     driver = driver + jnp.dot(state[1], part, preferred_element_type=jnp.float32)
-                value = (trade[9:10, :] * (jnp.exp(drift_rate * driver) - trade[10:11, :])).astype(jnp.bfloat16)
+                value = (notional[...] * (jnp.exp(drift_rate * driver) - strike[...])).astype(jnp.bfloat16)
                 sums = sums + lax.dot_general(
                     members[half], value, (((1,), (1,)), ((), ())), preferred_element_type=jnp.float32
                 )
             for t in range(2):
                 args[t, low, :] = totals[t]
-            net[:, :, low] = sums.astype(jnp.bfloat16).reshape(net.shape[0], SET_ROWS, chunk)
-
-
-def mix(lines, load_own, load_mate, proj_own, proj_mate, trade_own, trade_mate, n):
-    rows, factors = load_own.shape
+                largest = jnp.maximum(largest, jnp.max(jnp.abs(totals[t])))
+            sums_of.append(sums.reshape(net.shape[0], NSET_DEV, chunk))
+        net[...] = jnp.concatenate(sums_of, axis=1).astype(jnp.bfloat16)
+        unit = jnp.full(scale.shape, jnp.maximum(largest, 1e-30) * (1.0 / CODES), jnp.float32)
+        scale[...] = unit
+        inverse = 1.0 / unit[:1, :1]
+        span = codes.shape[1] // 2
+        for pair in range(codes.shape[0]):
+            piece = jnp.concatenate([args[t, pair * span : (pair + 1) * span, :] for t in range(2)], axis=0)
+            codes[pair] = encode(piece * inverse)
+
+
+def mix(lines, own, mate, n):
+    rows, factors = own[-1].shape
     width = 512
-    basis = proj_own.shape[1]
-    fixed = lambda j: (0, 0)
+    basis = own[-2].shape[1]
+    pairs = n // SHARE
+    codes_shape = (pairs, 2 * LOCAL // pairs, basis)
+    net_shape = (n, NSET_DEV * LOCAL // CHUNK, CHUNK)
+    loads = pl.BlockSpec((rows, width), lambda j: (0, j))
+    side = [pl.BlockSpec(array.shape, lambda j: (0, 0)) for array in own[:-1]] + [loads]
     return pl.pallas_call(
         mix_kernel,
         grid=(factors // width,),
         out_shape=(
-            jax.ShapeDtypeStruct((2, LOCAL, basis), jnp.float32),
-            jax.ShapeDtypeStruct((n, SET_ROWS, LOCAL), jnp.bfloat16),
+            jax.ShapeDtypeStruct(codes_shape, jnp.int16),
+            jax.ShapeDtypeStruct((8, 128), jnp.float32),
+            jax.ShapeDtypeStruct(net_shape, jnp.bfloat16),
         ),
-        in_specs=[
-            pl.BlockSpec((lines.shape[0], width), lambda j: (0, j)),
-            pl.BlockSpec((rows, width), lambda j: (0, j)),
-            pl.BlockSpec((rows, width), lambda j: (0, j)),
-            pl.BlockSpec(proj_own.shape, fixed),
-            pl.BlockSpec(proj_own.shape, fixed),
-            pl.BlockSpec(trade_own.shape, fixed),
-            pl.BlockSpec(trade_own.shape, fixed),
-        ],
+        in_specs=[pl.BlockSpec((lines.shape[0], width), lambda j: (0, j))] + side + side,
         out_specs=(
-            pl.BlockSpec((2, LOCAL, basis), lambda j: (0, 0, 0)),
-            pl.BlockSpec((n, SET_ROWS, LOCAL), lambda j: (0, 0, 0)),
+            pl.BlockSpec(codes_shape, lambda j: (0, 0, 0)),
+            pl.BlockSpec((8, 128), lambda j: (0, 0)),
+            pl.BlockSpec(net_shape, lambda j: (0, 0, 0)),
         ),
         scratch_shapes=[
             pltpu.VMEM((2 * LOCAL, width), jnp.bfloat16),
             pltpu.VMEM((POINTS, width), jnp.int32),
             pltpu.VMEM((2, 2 * LOCAL, rows), jnp.float32),
+            pltpu.VMEM((2, LOCAL, basis), jnp.float32),
         ],
         compiler_params=pltpu.CompilerParams(vmem_limit_bytes=VMEM_LIMIT),
-    )(lines, load_own, load_mate, proj_own, proj_mate, trade_own, trade_mate)
-
-
-def reduce_kernel(n, args, bias, net, phi, net_out, args_in, arg_sends, arg_recvs, net_sends, net_recvs, phi_sends, phi_recvs, mate_sends, mate_recvs, own):
+    )(lines, *own, *mate)
+
+
+def reduce_kernel(n, codes, scale, bias, net, phi, net_out, codes_in, scales_in, arg_sends, arg_recvs, scale_sends, scale_recvs, net_sends, net_recvs, phi_sends, phi_recvs, mate_sends, mate_recvs, own):
     me = lax.axis_index("fac")
     core = lax.rem(me, SHARE)
     pair = lax.div(me, SHARE)
     mate = me + 1 - 2 * core
     pairs = n // SHARE
-    block = LOCAL // pairs
     greet(me, n)
-
-    def part(index):
-        return pl.ds(pl.multiple_of(index * block, 8), block)
-
-    def place(index, side):
-        return pl.ds(pl.multiple_of(side * LOCAL + index * block, 8), block)
 
     arg_copies = []
     for step in range(1, pairs):
         other = lax.rem(pair + step, pairs)
-        arg_copies.append(
-            remote(args.at[:, part(other), :], args_in.at[pair], arg_sends.at[step], arg_recvs.at[step], SHARE * other + core)
-        )
+        peer = SHARE * other + core
+        arg_copies.append(remote(scale, scales_in.at[pair], scale_sends.at[step], scale_recvs.at[step], peer))
+        arg_copies.append(remote(codes.at[other], codes_in.at[pair], arg_sends.at[step], arg_recvs.at[step], peer))
     net_copies = []
     for step in range(1, n):
         peer = lax.rem(me + step, n)
@@ -260,26 +277,24 @@
         copy.start()
     keep = pltpu.make_async_copy(net.at[me], net_out.at[me], own)
     keep.start()
-    total = args[:, part(pair), :] + bias[...][None]
+    total = decode(codes[pair]) * scale[:1, :1] + bias[...]
     for copy in arg_copies:
         copy.wait_recv()
     for step in range(1, pairs):
-        total = total + args_in[lax.rem(pair + step, pairs)]
-    mine = place(pair, core)
-    phi[:, mine, :] = jnp.tanh(total)
+        other = lax.rem(pair + step, pairs)
+        total = total + decode(codes_in[other]) * scales_in[other][:1, :1]
+    phi[me] = encode(jnp.tanh(total) * CODES)
     phi_copies = []
     for step in range(1, pairs):
-        other = lax.rem(pair + step, pairs)
-        phi_copies.append(
-            remote(phi.at[:, mine, :], phi.at[:, mine, :], phi_sends.at[step], phi_recvs.at[step], SHARE * other + core)
-        )
-    mate_copies = [remote(phi.at[:, mine, :], phi.at[:, mine, :], mate_sends.at[0], mate_recvs.at[0], mate)]
+        peer = SHARE * lax.rem(pair + step, pairs) + core
+        phi_copies.append(remote(phi.at[me], phi.at[me], phi_sends.at[step], phi_recvs.at[step], peer))
+    mate_copies = [remote(phi.at[me], phi.at[me], mate_sends.at[0], mate_recvs.at[0], mate)]
     for copy in phi_copies + mate_copies:
         copy.start()
     for step in range(1, pairs):
         phi_copies[step - 1].wait_recv()
-        there = place(lax.rem(pair - step + pairs, pairs), core)
-        forward = remote(phi.at[:, there, :], phi.at[:, there, :], mate_sends.at[step], mate_recvs.at[step], mate)
+        there = SHARE * lax.rem(pair - step + pairs, pairs) + core
+        forward = remote(phi.at[there], phi.at[there], mate_sends.at[step], mate_recvs.at[step], mate)
         forward.start()
         mate_copies.append(forward)
     keep.wait()
@@ -291,36 +306,42 @@
         copy.wait_send()
 
 
-def reduce(args, bias, net):
+def reduce(codes, scale, bias, net):
     n = net.shape[0]
     pairs = n // SHARE
-    block = LOCAL // pairs
-    basis = args.shape[2]
     vmem = pl.BlockSpec(memory_space=pltpu.VMEM)
-    sems = [pltpu.SemaphoreType.DMA((k,)) for k in (pairs, pairs, n, n, pairs, pairs, pairs, pairs)]
+    sems = [pltpu.SemaphoreType.DMA((k,)) for k in (pairs, pairs, pairs, pairs, n, n, pairs, pairs, pairs, pairs)]
     return pl.pallas_call(
         functools.partial(reduce_kernel, n),
         out_shape=(
-            jax.ShapeDtypeStruct((2, SCENARIOS, basis), jnp.float32),
+            jax.ShapeDtypeStruct((n,) + codes.shape[1:], codes.dtype),
             jax.ShapeDtypeStruct(net.shape, net.dtype),
         ),
-        in_specs=[vmem] * 3,
+        in_specs=[vmem] * 4,
         out_specs=(vmem, vmem),
-        scratch_shapes=[pltpu.VMEM((pairs, 2, block, basis), jnp.float32)] + sems + [pltpu.SemaphoreType.DMA],
+        scratch_shapes=[pltpu.VMEM(codes.shape, codes.dtype), pltpu.VMEM((pairs, 8, 128), jnp.float32)]
+        + sems
+        + [pltpu.SemaphoreType.DMA],
         compiler_params=pltpu.CompilerParams(collective_id=1, has_side_effects=True, vmem_limit_bytes=VMEM_LIMIT),
-    )(args, bias, net)
-
-
-def regress_kernel(phi, net, fitted, exposure):
+    )(codes, scale, bias, net)
+
+
+def regress_kernel(phi_codes, net, fitted, exposure, phi):
     n = net.shape[0]
     basis = phi.shape[2]
-    sides = []
+    span = phi_codes.shape[1] // 2
+    for index in range(n):
+        piece = decode(phi_codes[index]) * (1.0 / CODES)
+        start = (index % SHARE) * LOCAL + (index // SHARE) * span
+        for t in range(2):
+            phi[t, start : start + span, :] = piece[t * span : (t + 1) * span]
+    parts = []
     for core in range(SHARE):
         side = net[core].astype(jnp.float32)
         for pair in range(1, n // SHARE):
             side = side + net[SHARE * pair + core].astype(jnp.float32)
-        sides.append(side)
-    netting = jnp.concatenate(sides, axis=1)
+        parts += [side[m * NSET_DEV : (m + 1) * NSET_DEV] for m in range(LOCAL // CHUNK)]
+    netting = jnp.concatenate(parts, axis=1)
     eye = jnp.where(
         lax.broadcasted_iota(jnp.int32, (basis, basis), 0) == lax.broadcasted_iota(jnp.int32, (basis, basis), 1),
         1.0,
@@ -352,7 +373,7 @@
         coeffs = coeffs + dot(rhs[t] - dot(coeffs, grams[t]), inverses[t])
         values = lax.dot_general(
             coeffs, phi[t], (((1,), (1,)), ((), ())), precision=HIGH, preferred_element_type=jnp.float32
-        )[:NSET_DEV]
+        )
         fitted[t] = values
         exposure[:, t : t + 1] = jnp.sum(jnp.maximum(values, 0.0), axis=1, keepdims=True) * (1.0 / SCENARIOS)
 
@@ -367,6 +388,7 @@
         ),
         in_specs=[vmem] * 2,
         out_specs=(vmem, vmem),
+        scratch_shapes=[pltpu.VMEM((2, SCENARIOS, phi.shape[2]), jnp.float32)],
         compiler_params=pltpu.CompilerParams(vmem_limit_bytes=VMEM_LIMIT),
     )(phi, net)
 
@@ -395,13 +417,12 @@
         ],
         axis=0,
     )
-    sets = trade_owner[:, 0] * SET_ROWS + trade_slot
-    extra = jnp.stack([trade_block.astype(jnp.float32), trade_notional, trade_strike, sets.astype(jnp.float32)])
-    trade = jnp.concatenate([trade_weights.T, extra, jnp.zeros_like(extra)], axis=0)
-    all_lines, load_mate, proj_mate, trade_mate = share(lines, loading, basis_proj, trade, n)
+    trades = [array.reshape(1, -1) for array in (trade_block, trade_slot, trade_owner, trade_notional, trade_strike)]
+    own = trades + [trade_weights.T, basis_proj, loading]
+    all_lines, *mate = share(lines, own, n)
     all_lines = jnp.transpose(all_lines, (1, 0, 2)).reshape(2 * LINES, factors)
-    args, net = mix(all_lines, loading, load_mate, basis_proj, proj_mate, trade, trade_mate, n)
-    phi, net = reduce(args, basis_bias[None, :], net)
+    codes, scale, net = mix(all_lines, own, mate, n)
+    phi, net = reduce(codes, scale, basis_bias[None, :], net)
     return regress(phi, net)
 
 

time: 153 us -> 126 us (0.82)
  Pallas kernels: 141 us -> 114 us
  other arithmetic: 2.7 us -> 0.64 us
  local copies, waits for them, and re-layouts: 8.18 us -> 9.96 us
    pallas_call x1, Pallas kernels: 66.4 us -> 41.1 us  [reduce(): pl.pallas_call(functools.partial(reduce_kernel, n), out_shape=(jax.ShapeD...]
    reshape x0 -> x4, local copies, waits for them, and re-layouts: none -> 5.08 us  [local(): array.reshape(1, -1)]
    concatenate x1 -> x0, local copies, waits for them, and re-layouts: 1.92 us -> none  [local(): jnp.concatenate([trade_weights.T, extra, jnp.zeros_like(extra)], axis=0)]
    pallas_call x1, Pallas kernels: 21.2 us -> 19.5 us  [regress(): pl.pallas_call(regress_kernel, out_shape=(jax.ShapeDtypeStruct((2, NSET_D...]
where the time goes in v2:
time: 126 us
  Pallas kernels  114 us (90%)
  local copies, waits for them, and re-layouts  9.96 us (8%)
    pallas_call x1, Pallas kernels, reduce(): pl.pallas_call(functools.partial(reduce_kernel, n), out_shape=(jax.ShapeD...  41.1 us
    pallas_call x1, Pallas kernels, mix(): pl.pallas_call(mix_kernel, grid=(factors // width,), out_shape=(jax.Shape...  39.6 us
    pallas_call x1, Pallas kernels, regress(): pl.pallas_call(regress_kernel, out_shape=(jax.ShapeDtypeStruct((2, NSET_D...  19.5 us
    pallas_call x1, Pallas kernels, share(): pl.pallas_call(functools.partial(share_kernel, n), out_shape=[jax.ShapeDt...  14.1 us
    reshape x4, local copies, waits for them, and re-layouts, local(): array.reshape(1, -1)  5.08 us

profile of v2, /device:TPU:27, one launch (start us, length us, event | category | flops | bytes accessed | tf_op | source)
XLA Modules:
  0.0 125.5 jit_solution(3945303368687935218)
XLA Ops:
  0.6 1.3 %reshape.30.refs_1_.refs_0_ = s32[1,320]{1,0:T(1,128)} reshape(s32[320]{0:T(512)} %param.16) | data formatting | bytes 2560 | tf_op jit(solution)/shard_map/reshape | solution.py:420
  1.9 1.3 %reshape.33.refs_4_.refs_3_ = f32[1,320]{1,0:T(1,128)} reshape(f32[320]{0:T(512)} %param.18) | data formatting | bytes 2560 | tf_op jit(solution)/shard_map/reshape | solution.py:420
  3.2 1.3 %reshape.34.refs_5_.refs_4_ = f32[1,320]{1,0:T(1,128)} reshape(f32[320]{0:T(512)} %param.19) | data formatting | bytes 2560 | tf_op jit(solution)/shard_map/reshape | solution.py:420
  4.4 1.3 %reshape.31.refs_2_.refs_1_ = s32[1,320]{1,0:T(1,128)} reshape(s32[320]{0:T(512)} %param.21) | data formatting | bytes 2560 | tf_op jit(solution)/shard_map/reshape | solution.py:420
  5.7 0.7 copy.15
  6.4 0.7 fusion
  7.2 0.6 pad_add_fusion.refs_0_
  7.8 14.1 %shard_map.122 = (s32[16,18,256]{2,1,0:T(8,128)}, s32[1,320]{1,0:T(1,128)}, s32[1,320]{1,0:T(1,128)}, s32[1,320]{1,0:T(1,128)}, f32[1,320]{1,0:T(1,128)}, /*inde...) custom-call(s32[2,18,256]{2,1,0:T(8,128)} %pad_add_fusion.refs_0_, ...), custom_call_target="tpu_custom_call" | custom-call | tf_op jit(solution)/shard_map/pallas_call | solution.py:109
  21.9 1.1 copy.17
  23.0 1.0 copy.19
  24.0 39.6 %shard_map.123 = (s16[8,128,256]{2,1,0:T(8,128)(2,1)}, f32[8,128]{1,0:T(8,128)}, bf16[16,96,128]{2,1,0:T(8,128)(2,1)}) custom-call(s32[18,4096]{1,0:T(8,128)} %bitcast.8, s32[1,320]{1,0:T(1,128)} %reshape.30.refs_1_.refs_0_, s32[1,320]{1,0:T(1,128)} %reshape.31.refs_2_.refs_1_, s32[1,320]{1,0:T(1,128)} %bitcast.14, f32[1,320]{1,0:T(1,128)} %reshape.33.refs_4_.refs_3_, ...), custom_call_target="tpu_custom_call" | custom-call | tf_op jit(solution)/shard_map/pallas_call | solution.py:234
  63.6 41.1 %shard_map.124 = (s16[16,128,256]{2,1,0:T(8,128)(2,1)}, bf16[16,96,128]{2,1,0:T(8,128)(2,1)}) custom-call(s16[8,128,256]{2,1,0:T(8,128)(2,1)} %get-tuple-element.25.codes, f32[8,128]{1,0:T(8,128)} %get-tuple-element.26.scale, f32[1,256]{1,0:T(1,128)} %bitcast.16, bf16[16,96,128]{2,1,0:T(8,128)(2,1)} %get-tuple-element.27.net), custom_call_target="tpu_custom_call" | custom-call | tf_op jit(solution)/shard_map/pallas_call | solution.py:314
  104.7 19.5 %shard_map.125 = (f32[2,24,1024]{2,1,0:T(8,128)}, f32[24,2]{1,0:T(8,128)}) custom-call(s16[16,128,256]{2,1,0:T(8,128)(2,1)} %get-tuple-element.28.phi_codes, bf16[16,96,128]{2,1,0:T(8,128)(2,1)} %get-tuple-element.29.net), custom_call_target="tpu_custom_call" | custom-call | tf_op jit(solution)/shard_map/pallas_call | solution.py:383
  124.2 1.3 %copy.18 = f32[24,2]{0,1:T(2,128)} copy(f32[24,2]{1,0:T(8,128)} %get-tuple-element.33) | data formatting | bytes 384 | tf_op jit(solution)/shard_map/pallas_call | solution.py:383
  (4 shorter events, 0.1 us)

commit v3 on v2

--- a/solution.py
+++ b/solution.py
@@ -17,7 +17,6 @@
 SCENARIOS = REPLICAS * POINTS
 LOCAL = SCENARIOS // SHARE
 LOCAL_REPLICAS = REPLICAS // SHARE
-LINES = 1 + LOCAL_REPLICAS
 
 drift_rate = 0.25
 ridge_term = 0.01
@@ -79,108 +78,147 @@
 
 def share_kernel(n, *refs):
     count = (len(refs) - 5) // 2
-    lines, *mine = refs[:count]
-    lines_out, *theirs = refs[count : 2 * count]
+    gen, shift, *mine = refs[:count]
+    gen_out, shift_out, *theirs = refs[count : 2 * count]
     sends, recvs, mate_sends, mate_recvs, own = refs[2 * count :]
     me = lax.axis_index("fac")
     core = lax.rem(me, SHARE)
     mate = me + 1 - 2 * core
+    width = gen.shape[1]
+    if len(gen_out.shape) == 2:
+        columns = pl.ds(pl.multiple_of(me * width, 128), width)
+        gen_to, shift_to = gen_out.at[:, columns], shift_out.at[:, :, columns]
+    else:
+        gen_to, shift_to = gen_out.at[me], shift_out.at[me]
+
+    def replicas(side):
+        return shift.at[:, pl.ds(pl.multiple_of(side * LOCAL_REPLICAS, LOCAL_REPLICAS), LOCAL_REPLICAS), :]
+
     greet(me, n)
     copies = []
     for step in range(1, n):
         peer = lax.rem(me + step, n)
-        copies.append(
-            remote(lines.at[lax.rem(peer, SHARE)], lines_out.at[me], sends.at[step], recvs.at[step], peer)
-        )
+        copies.append(remote(gen, gen_to, sends.at[0, step], recvs.at[0, step], peer))
+        copies.append(remote(replicas(lax.rem(peer, SHARE)), shift_to, sends.at[1, step], recvs.at[1, step], peer))
     for index, (src, dst) in enumerate(zip(mine, theirs)):
         copies.append(remote(src, dst, mate_sends.at[index], mate_recvs.at[index], mate))
     for copy in copies:
         copy.start()
-    keep = pltpu.make_async_copy(lines.at[core], lines_out.at[me], own)
-    keep.start()
-    keep.wait()
-    for copy in copies:
+    keeps = [
+        pltpu.make_async_copy(gen, gen_to, own.at[0]),
+        pltpu.make_async_copy(replicas(core), shift_to, own.at[1]),
+    ]
+    for keep in keeps:
+        keep.start()
+    for copy in keeps + copies:
         copy.wait()
 
 
-def share(lines, arrays, n):
+def share(gen, shift, arrays, n):
     hbm = pl.BlockSpec(memory_space=pl.ANY)
     count = len(arrays)
-    return pl.pallas_call(
+    width = gen.shape[1]
+    whole = width % 128 == 0
+    if whole:
+        shapes = [(2, n * width), (2, LOCAL_REPLICAS, n * width)]
+    else:
+        shapes = [(n, 2, width), (n, 2, LOCAL_REPLICAS, width)]
+    all_gen, all_shift, *mate = pl.pallas_call(
         functools.partial(share_kernel, n),
-        out_shape=[jax.ShapeDtypeStruct((n,) + lines.shape[1:], lines.dtype)]
+        out_shape=[jax.ShapeDtypeStruct(shape, gen.dtype) for shape in shapes]
         + [jax.ShapeDtypeStruct(array.shape, array.dtype) for array in arrays],
-        in_specs=[hbm] * (count + 1),
-        out_specs=[hbm] * (count + 1),
+        in_specs=[hbm] * (count + 2),
+        out_specs=[hbm] * (count + 2),
         scratch_shapes=[
-            pltpu.SemaphoreType.DMA((n,)),
-            pltpu.SemaphoreType.DMA((n,)),
+            pltpu.SemaphoreType.DMA((2, n)),
+            pltpu.SemaphoreType.DMA((2, n)),
             pltpu.SemaphoreType.DMA((count,)),
             pltpu.SemaphoreType.DMA((count,)),
-            pltpu.SemaphoreType.DMA,
+            pltpu.SemaphoreType.DMA((2,)),
         ],
         compiler_params=pltpu.CompilerParams(collective_id=0, has_side_effects=True),
-    )(lines, *arrays)
-
-
-def mix_kernel(lines, *refs):
+    )(gen, shift, *arrays)
+    if not whole:
+        all_gen = jnp.transpose(all_gen, (1, 0, 2)).reshape(2, n * width)
+        all_shift = jnp.transpose(all_shift, (1, 2, 0, 3)).reshape(2, LOCAL_REPLICAS, n * width)
+    return all_gen, all_shift, mate
+
+
+def mix_kernel(gen, shift, *refs):
     own, mate = refs[:8], refs[8:16]
-    codes, scale, net, normal, base, mixed, args = refs[16:]
+    codes, scale, net, even, odd, base, mixed, args = refs[16:]
     load_own, load_mate = own[-1], mate[-1]
     step = pl.program_id(0)
-    width = lines.shape[1]
+    last = pl.num_programs(0) - 1
+    width = gen.shape[1]
     rows = load_own.shape[0]
     tile = 16
+    group = 4
+    span = group * POINTS
 
     @pl.when(step == 0)
     def _():
         mixed[...] = jnp.zeros_like(mixed)
-
-    for t in range(2):
-        base[...] = lax.broadcasted_iota(jnp.int32, (POINTS, width), 0) * lines[t * LINES : t * LINES + 1, :]
-
-        def replica(r, carry):
-            shift = lines[pl.ds(t * LINES + 1 + r, 1), :]
-            for part in range(POINTS // tile):
-                index = (base[part * tile : (part + 1) * tile, :] + shift) & (LATTICE - 1)
-                x = index.astype(jnp.float32) * (2.0 / LATTICE) + (1.0 / LATTICE - 1.0)
-                power = jnp.log((1.0 - x) * (1.0 + x)) * LOG_SCALE - 1.0
-                ratio = power * NORMAL_TERMS[-1] + NORMAL_TERMS[-2]
-                for term in NORMAL_TERMS[-3::-1]:
-                    ratio = ratio * power + term
-                start = pl.multiple_of(t * LOCAL + r * POINTS + part * tile, tile)
-                normal[pl.ds(start, tile), :] = (ratio * x).astype(jnp.bfloat16)
+        odd[...] = jnp.zeros_like(odd)
+
+    def draw(into, t, r, place):
+        offsets = shift[t, pl.ds(r, 1), :]
+        for part in range(POINTS // tile):
+            index = (base[t, part * tile : (part + 1) * tile, :] + offsets) & (LATTICE - 1)
+            x = index.astype(jnp.float32) * (2.0 / LATTICE) + (1.0 / LATTICE - 1.0)
+            power = jnp.log((1.0 - x) * (1.0 + x)) * LOG_SCALE - 1.0
+            ratio = power * NORMAL_TERMS[-1] + NORMAL_TERMS[-2]
+            for term in NORMAL_TERMS[-3::-1]:
+                ratio = ratio * power + term
+            into[pl.ds(pl.multiple_of(place + part * tile, tile), tile), :] = (ratio * x).astype(jnp.bfloat16)
+
+    def advance(into, source):
+        if into is not None:
+            points = lax.broadcasted_iota(jnp.int32, (POINTS, width), 0)
+            for t in range(2):
+                base[t] = points * gen[t : t + 1, :]
+
+        def some(m, carry):
+            start = pl.multiple_of(m * span, span)
+            left = source[pl.ds(start, span), :]
+            for half, load in enumerate((load_own, load_mate)):
+                mixed[half, pl.ds(start, span), :] += lax.dot_general(
+                    left, load[...], (((1,), (1,)), ((), ())), preferred_element_type=jnp.float32
+                )
+            if into is not None:
+                t = lax.div(m, LOCAL // span)
+                first = lax.rem(m, LOCAL // span) * group
+                for r in range(group):
+                    draw(into, t, first + r, start + r * POINTS)
             return carry
 
-        lax.fori_loop(0, LOCAL_REPLICAS, replica, 0)
-
-    def multiply(m, carry):
-        span = pl.ds(pl.multiple_of(m * 256, 256), 256)
-        left = normal[span, :]
-        for half, load in enumerate((load_own, load_mate)):
-            mixed[half, span, :] += lax.dot_general(
-                left, load[...], (((1,), (1,)), ((), ())), preferred_element_type=jnp.float32
-            )
-        return carry
-
-    lax.fori_loop(0, 2 * LOCAL // 256, multiply, 0)
-
-    @pl.when(step == pl.num_programs(0) - 1)
+        lax.fori_loop(0, 2 * LOCAL // span, some, 0)
+
+    @pl.when((step < last) & (lax.rem(step, 2) == 0))
     def _():
+        advance(even, odd)
+
+    @pl.when((step < last) & (lax.rem(step, 2) == 1))
+    def _():
+        advance(odd, even)
+
+    @pl.when(step == last)
+    def _():
+        advance(None, odd)
         picks = []
         members = []
         n_rows = net.shape[0] * NSET_DEV
         for block, slot, owner, _, _, weight, _, _ in (own, mate):
             weights = jnp.concatenate([weight[...]] * (rows // BLOCK), axis=0)
             home = lax.shift_right_logical(lax.broadcasted_iota(jnp.int32, weights.shape, 0), 3)
-            pick = jnp.where(home == block[...], weights, 0.0)
+            pick = jnp.where(home == block[...].reshape(1, -1), weights, 0.0)
             parts = []
             for _ in range(3):
                 part = pick.astype(jnp.bfloat16)
                 parts.append(part)
                 pick = pick - part.astype(jnp.float32)
             picks.append(parts)
-            sets = owner[...] * NSET_DEV + slot[...]
+            sets = owner[...] * NSET_DEV + slot[...].reshape(1, -1)
             members.append(
                 jnp.where(lax.broadcasted_iota(jnp.int32, (n_rows, sets.shape[1]), 0) == sets, 1.0, 0.0).astype(jnp.bfloat16)
             )
@@ -204,7 +242,7 @@
                 driver = 0.0
                 for part in picks[half]:
                     driver = driver + jnp.dot(state[1], part, preferred_element_type=jnp.float32)
-                value = (notional[...] * (jnp.exp(drift_rate * driver) - strike[...])).astype(jnp.bfloat16)
+                value = (notional[...].reshape(1, -1) * (jnp.exp(drift_rate * driver) - strike[...].reshape(1, -1))).astype(jnp.bfloat16)
                 sums = sums + lax.dot_general(
                     members[half], value, (((1,), (1,)), ((), ())), preferred_element_type=jnp.float32
                 )
@@ -222,24 +260,31 @@
             codes[pair] = encode(piece * inverse)
 
 
-def mix(lines, own, mate, n):
+def mix(gen, shift, own, mate, n):
     rows, factors = own[-1].shape
     width = 512
     basis = own[-2].shape[1]
     pairs = n // SHARE
     codes_shape = (pairs, 2 * LOCAL // pairs, basis)
     net_shape = (n, NSET_DEV * LOCAL // CHUNK, CHUNK)
-    loads = pl.BlockSpec((rows, width), lambda j: (0, j))
-    side = [pl.BlockSpec(array.shape, lambda j: (0, 0)) for array in own[:-1]] + [loads]
+    steps = factors // width
+    assert steps % 2 == 0
+    loads = pl.BlockSpec((rows, width), lambda j: (0, jnp.maximum(j - 1, 0)))
+    side = [pl.BlockSpec(array.shape, functools.partial(lambda ndim, j: (0,) * ndim, array.ndim)) for array in own[:-1]] + [loads]
     return pl.pallas_call(
         mix_kernel,
-        grid=(factors // width,),
+        grid=(steps + 1,),
         out_shape=(
             jax.ShapeDtypeStruct(codes_shape, jnp.int16),
             jax.ShapeDtypeStruct((8, 128), jnp.float32),
             jax.ShapeDtypeStruct(net_shape, jnp.bfloat16),
         ),
-        in_specs=[pl.BlockSpec((lines.shape[0], width), lambda j: (0, j))] + side + side,
+        in_specs=[
+            pl.BlockSpec((2, width), lambda j: (0, jnp.minimum(j, steps - 1))),
+            pl.BlockSpec((2, LOCAL_REPLICAS, width), lambda j: (0, 0, jnp.minimum(j, steps - 1))),
+        ]
+        + side
+        + side,
         out_specs=(
             pl.BlockSpec(codes_shape, lambda j: (0, 0, 0)),
             pl.BlockSpec((8, 128), lambda j: (0, 0)),
@@ -247,12 +292,13 @@
         ),
         scratch_shapes=[
             pltpu.VMEM((2 * LOCAL, width), jnp.bfloat16),
-            pltpu.VMEM((POINTS, width), jnp.int32),
+            pltpu.VMEM((2 * LOCAL, width), jnp.bfloat16),
+            pltpu.VMEM((2, POINTS, width), jnp.int32),
             pltpu.VMEM((2, 2 * LOCAL, rows), jnp.float32),
             pltpu.VMEM((2, LOCAL, basis), jnp.float32),
         ],
         compiler_params=pltpu.CompilerParams(vmem_limit_bytes=VMEM_LIMIT),
-    )(lines, *own, *mate)
+    )(gen, shift, *own, *mate)
 
 
 def reduce_kernel(n, codes, scale, bias, net, phi, net_out, codes_in, scales_in, arg_sends, arg_recvs, scale_sends, scale_recvs, net_sends, net_recvs, phi_sends, phi_recvs, mate_sends, mate_recvs, own):
@@ -407,21 +453,18 @@
     trade_slot,
 ):
     n = lax.axis_size("fac")
-    factors = loading.shape[1]
-    lines = jnp.concatenate(
-        [
-            jnp.concatenate(
-                [lattice_gen[:, None, :], lattice_shift[:, side * LOCAL_REPLICAS : (side + 1) * LOCAL_REPLICAS, :]], axis=1
-            ).reshape(1, 2 * LINES, -1)
-            for side in range(SHARE)
-        ],
-        axis=0,
-    )
-    trades = [array.reshape(1, -1) for array in (trade_block, trade_slot, trade_owner, trade_notional, trade_strike)]
-    own = trades + [trade_weights.T, basis_proj, loading]
-    all_lines, *mate = share(lines, own, n)
-    all_lines = jnp.transpose(all_lines, (1, 0, 2)).reshape(2 * LINES, factors)
-    codes, scale, net = mix(all_lines, own, mate, n)
+    own = [
+        trade_block,
+        trade_slot,
+        trade_owner.reshape(1, -1),
+        trade_notional,
+        trade_strike,
+        trade_weights.T,
+        basis_proj,
+        loading,
+    ]
+    gen, shift, mate = share(lattice_gen, lattice_shift, own, n)
+    codes, scale, net = mix(gen, shift, own, mate, n)
     phi, net = reduce(codes, scale, basis_bias[None, :], net)
     return regress(phi, net)
 

time: 126 us -> 105 us (0.83)
  Pallas kernels: 114 us -> 103 us
  local copies, waits for them, and re-layouts: 9.96 us -> 1.34 us
    pallas_call x1, Pallas kernels: 39.6 us -> 29.7 us  [mix(): pl.pallas_call(mix_kernel, grid=(steps + 1,), out_shape=(jax.ShapeDtypeSt...]
    reshape x6 -> x0, local copies, waits for them, and re-layouts: 5.09 us -> none  [the longest x4 5.08 us: local(): array.reshape(1, -1)]
    pallas_call x1, Pallas kernels: 14.1 us -> 12.5 us  [share(): pl.pallas_call(functools.partial(share_kernel, n), out_shape=[jax.ShapeDt...]
where the time goes in v3:
time: 105 us
  Pallas kernels  103 us (98%)
  local copies, waits for them, and re-layouts  1.34 us (1%)
    pallas_call x1, Pallas kernels, reduce(): pl.pallas_call(functools.partial(reduce_kernel, n), out_shape=(jax.ShapeD...  41.1 us
    pallas_call x1, Pallas kernels, mix(): pl.pallas_call(mix_kernel, grid=(steps + 1,), out_shape=(jax.ShapeDtypeSt...  29.7 us
    pallas_call x1, Pallas kernels, regress(): pl.pallas_call(regress_kernel, out_shape=(jax.ShapeDtypeStruct((2, NSET_D...  19.5 us
    pallas_call x1, Pallas kernels, share(): pl.pallas_call(functools.partial(share_kernel, n), out_shape=[jax.ShapeDt...  12.5 us

profile of v3, /device:TPU:27, one launch (start us, length us, event | category | flops | bytes accessed | tf_op | source)
XLA Modules:
  0.0 104.8 jit_solution(17869331342409782568)
XLA Ops:
  0.6 12.5 %shard_map.122 = (s32[2,4096]{1,0:T(2,128)}, s32[2,8,4096]{2,1,0:T(8,128)}, s32[320]{0:T(512)}, s32[320]{0:T(512)}, s32[1,320]{1,0:T(1,128)}, /*index=5*/f32[320...) custom-call(s32[2,256]{1,0:T(2,128)} %refs_0_.2, ...), custom_call_target="tpu_custom_call" | custom-call | tf_op jit(solution)/shard_map/pallas_call | solution.py:126
  13.1 29.7 %shard_map.123 = (s16[8,128,256]{2,1,0:T(8,128)(2,1)}, f32[8,128]{1,0:T(8,128)}, bf16[16,96,128]{2,1,0:T(8,128)(2,1)}) custom-call(s32[2,4096]{1,0:T(2,128)} %get-tuple-element.17.gen, s32[2,8,4096]{2,1,0:T(8,128)} %get-tuple-element.18.shift, s32[320]{0:T(512)} %refs_0_.3, s32[320]{0:T(512)} %refs_1_.3, s32[1,320]{1,0:T(1,128)} %bitcast.6, f32[320]{0:T(512)} %refs_3_.3, ...), custom_call_target="tpu_custom_call" | custom-call | tf_op jit(solution)/shard_map/pallas_call | solution.py:274
  42.8 41.1 %shard_map.124 = (s16[16,128,256]{2,1,0:T(8,128)(2,1)}, bf16[16,96,128]{2,1,0:T(8,128)(2,1)}) custom-call(s16[8,128,256]{2,1,0:T(8,128)(2,1)} %get-tuple-element.27.codes, f32[8,128]{1,0:T(8,128)} %get-tuple-element.28.scale, f32[1,256]{1,0:T(1,128)} %bitcast.7, bf16[16,96,128]{2,1,0:T(8,128)(2,1)} %get-tuple-element.29.net), custom_call_target="tpu_custom_call" | custom-call | tf_op jit(solution)/shard_map/pallas_call | solution.py:360
  83.9 19.5 %shard_map.125 = (f32[2,24,1024]{2,1,0:T(8,128)}, f32[24,2]{1,0:T(8,128)}) custom-call(s16[16,128,256]{2,1,0:T(8,128)(2,1)} %get-tuple-element.30.phi_codes, bf16[16,96,128]{2,1,0:T(8,128)(2,1)} %get-tuple-element.31.net), custom_call_target="tpu_custom_call" | custom-call | tf_op jit(solution)/shard_map/pallas_call | solution.py:429
  103.5 1.3 %copy.13 = f32[24,2]{0,1:T(2,128)} copy(f32[24,2]{1,0:T(8,128)} %get-tuple-element.33) | data formatting | bytes 384 | tf_op jit(solution)/shard_map/pallas_call | solution.py:429

commit v4 on v3

--- a/solution.py
+++ b/solution.py
@@ -319,13 +319,15 @@
     for step in range(1, n):
         peer = lax.rem(me + step, n)
         net_copies.append(remote(net.at[peer], net_out.at[me], net_sends.at[step], net_recvs.at[step], peer))
-    for copy in arg_copies + net_copies:
+    for copy in arg_copies:
         copy.start()
     keep = pltpu.make_async_copy(net.at[me], net_out.at[me], own)
     keep.start()
     total = decode(codes[pair]) * scale[:1, :1] + bias[...]
     for copy in arg_copies:
         copy.wait_recv()
+    for copy in net_copies:
+        copy.start()
     for step in range(1, pairs):
         other = lax.rem(pair + step, pairs)
         total = total + decode(codes_in[other]) * scales_in[other][:1, :1]

time: 105 us -> 107 us (1.019)
    pallas_call x1, Pallas kernels: 41.1 us -> 42.7 us  [reduce(): pl.pallas_call(functools.partial(reduce_kernel, n), out_shape=(jax.ShapeD...]
where the time goes in v4:
time: 107 us; the launch traced here: 106 us
  Pallas kernels  104 us (97%)
  local copies, waits for them, and re-layouts  1.34 us (1%)
    pallas_call x1, Pallas kernels, reduce(): pl.pallas_call(functools.partial(reduce_kernel, n), out_shape=(jax.ShapeD...  42.7 us
    pallas_call x1, Pallas kernels, mix(): pl.pallas_call(mix_kernel, grid=(steps + 1,), out_shape=(jax.ShapeDtypeSt...  29.7 us
    pallas_call x1, Pallas kernels, regress(): pl.pallas_call(regress_kernel, out_shape=(jax.ShapeDtypeStruct((2, NSET_D...  19.5 us
    pallas_call x1, Pallas kernels, share(): pl.pallas_call(functools.partial(share_kernel, n), out_shape=[jax.ShapeDt...  12.5 us

profile of v4, /device:TPU:27, one launch (start us, length us, event | category | flops | bytes accessed | tf_op | source)
XLA Modules:
  0.0 106.4 jit_solution(5161173057552523441)
XLA Ops:
  0.6 12.5 %shard_map.122 = (s32[2,4096]{1,0:T(2,128)}, s32[2,8,4096]{2,1,0:T(8,128)}, s32[320]{0:T(512)}, s32[320]{0:T(512)}, s32[1,320]{1,0:T(1,128)}, /*index=5*/f32[320...) custom-call(s32[2,256]{1,0:T(2,128)} %refs_0_.2, ...), custom_call_target="tpu_custom_call" | custom-call | tf_op jit(solution)/shard_map/pallas_call | solution.py:126
  13.1 29.7 %shard_map.123 = (s16[8,128,256]{2,1,0:T(8,128)(2,1)}, f32[8,128]{1,0:T(8,128)}, bf16[16,96,128]{2,1,0:T(8,128)(2,1)}) custom-call(s32[2,4096]{1,0:T(2,128)} %get-tuple-element.17.gen, s32[2,8,4096]{2,1,0:T(8,128)} %get-tuple-element.18.shift, s32[320]{0:T(512)} %refs_0_.3, s32[320]{0:T(512)} %refs_1_.3, s32[1,320]{1,0:T(1,128)} %bitcast.6, f32[320]{0:T(512)} %refs_3_.3, ...), custom_call_target="tpu_custom_call" | custom-call | tf_op jit(solution)/shard_map/pallas_call | solution.py:274
  42.8 42.7 %shard_map.124 = (s16[16,128,256]{2,1,0:T(8,128)(2,1)}, bf16[16,96,128]{2,1,0:T(8,128)(2,1)}) custom-call(s16[8,128,256]{2,1,0:T(8,128)(2,1)} %get-tuple-element.27.codes, f32[8,128]{1,0:T(8,128)} %get-tuple-element.28.scale, f32[1,256]{1,0:T(1,128)} %bitcast.7, bf16[16,96,128]{2,1,0:T(8,128)(2,1)} %get-tuple-element.29.net), custom_call_target="tpu_custom_call" | custom-call | tf_op jit(solution)/shard_map/pallas_call | solution.py:362
  85.5 19.5 %shard_map.125 = (f32[2,24,1024]{2,1,0:T(8,128)}, f32[24,2]{1,0:T(8,128)}) custom-call(s16[16,128,256]{2,1,0:T(8,128)(2,1)} %get-tuple-element.30.phi_codes, bf16[16,96,128]{2,1,0:T(8,128)(2,1)} %get-tuple-element.31.net), custom_call_target="tpu_custom_call" | custom-call | tf_op jit(solution)/shard_map/pallas_call | solution.py:431
  105.1 1.3 %copy.13 = f32[24,2]{0,1:T(2,128)} copy(f32[24,2]{1,0:T(8,128)} %get-tuple-element.33) | data formatting | bytes 384 | tf_op jit(solution)/shard_map/pallas_call | solution.py:431
